TPU v7x, 32 devices: a whole 2x2x4 slice. The times are simulated.
32 devices in a mesh: inst: 8 (over z, core), tm: 4 (over y, x).
Axes of the slice: x: 2, y: 2, z: 4, core: 2. Of those that a mesh axis runs over, the one named last changes fastest.
Arguments:
- log_prices: bfloat16 [1536, 8192], P('tm', 'inst'), may hold values from -40 to 40
- scaling_filter: float32 [16], replicated, may hold values from -1.5 to 1.5
Outputs:
- variation: float32 [8192, 2, 8192], P('tm', None, 'inst')
All inputs are finite; a program needn't handle non-finite values.
Results may differ from a plain program's by a relative error of at most 0.0003.
Values may be sent and summed in bfloat16 or wider, within the bound.
A program may use at most 192 MiB of HBM per device.

v0:
```python
import jax
import jax.numpy as jnp
from jax import lax
from jax.sharding import PartitionSpec as P

TAPS = 16
LEVELS = 2


def from_behind(block, axis, distance):
    devices = range(lax.axis_size(axis))
    route = [((i - distance) % len(devices), i) for i in devices]
    return lax.ppermute(block, axis, route)


def apply_taps(extended, filter_taps, dilation, row_count):
    rim_rows = (TAPS - 1) * dilation
    running = filter_taps[0] * extended[rim_rows : rim_rows + row_count]
    for lag_index in range(1, TAPS):
        first_row = rim_rows - lag_index * dilation
        running = running + filter_taps[lag_index] * extended[first_row : first_row + row_count]
    return running


def per_level(series, low_pass, high_pass, slab_rows):
    smooth = series.astype(jnp.float32)
    details = []
    for level in range(LEVELS):
        dilation = 2**level
        rim_rows = (TAPS - 1) * dilation
        earlier = from_behind(smooth[-rim_rows:], "tm", 1)
        extended = jnp.concatenate([earlier, smooth], 0)
        details.append(apply_taps(extended, high_pass, dilation, slab_rows).astype(jnp.bfloat16))
        if level + 1 < LEVELS:
            smooth = apply_taps(extended, low_pass, dilation, slab_rows)
    return jnp.stack(details)


def per_device(log_prices, scaling_filter):
    slab_rows = log_prices.shape[0]
    own_count = log_prices.shape[1]
    alternating = jnp.where(jnp.arange(TAPS) % 2 == 0, 1.0, -1.0).astype(jnp.float32)
    high_pass = scaling_filter[::-1] * alternating
    own_coef = per_level(log_prices, scaling_filter, high_pass, slab_rows)
    all_coef = lax.all_gather(own_coef, "inst", axis=2, tiled=True)
    local_energy = jnp.sum(jnp.square(all_coef.astype(jnp.float32)), axis=1)
    energy = lax.psum(local_energy, "tm")
    col_count = all_coef.shape[2] // lax.axis_size("tm")
    gram_tile = lax.psum_scatter(
        jnp.einsum("jtc,jtr->cjr", all_coef, own_coef, preferred_element_type=jnp.float32),
        "tm",
        scatter_dimension=0,
        tiled=True,
    )
    col_energy = lax.dynamic_slice_in_dim(energy, lax.axis_index("tm") * col_count, col_count, 1)
    row_energy = lax.dynamic_slice_in_dim(energy, lax.axis_index("inst") * own_count, own_count, 1)
    tick_total = slab_rows * lax.axis_size("tm")
    return (
        jnp.transpose(col_energy)[:, :, None] + row_energy[None, :, :] - 2.0 * gram_tile
    ) / tick_total


def solution(mesh):
    placed = (P("tm", "inst"), P())
    return jax.shard_map(
        per_device, mesh=mesh, in_specs=placed, out_specs=P("tm", None, "inst"), check_vma=False
    )
```

profile of v0, /device:TPU:7, one launch (start us, length us, event | category | flops | bytes accessed | tf_op | source)
XLA Modules:
  0.0 825.1 jit_solution(12309921030237811918)
XLA Ops:
  6.5 0.0 all-gather.2.cloned.1.call-start
  6.5 0.8 slice.287
  7.3 0.1 collective-permute-start
  7.4 0.7 rev.3
  8.1 2.0 fusion.63
  10.1 1.3 convert_element_type.12
  11.4 0.7 fusion.62
  12.1 0.0 collective-permute-done
  12.1 13.1 %multiply_add_fusion = f32[384,1024]{1,0:T(8,128)S(1)} fusion(f32[384,1024]{1,0:T(8,128)S(1)} %convert_element_type.12, f32[15,1024]{1,0:T(8,128)S(1)} %collective-permute-done, f32[]{:T(128)} %bitcast.32, f32[]{:T(128)} %bitcast.31, f32[]{:T(128)} %bitcast.30, f32[]{:T(128)} %bitcast.29, f32[]{:T(128)} %bitcast.28, f32[]{:T(128)} %bitcast.27, f32[]{:T(128)} %bitcast.26, ...), kind=kLoop, calls=%fused_computation.105 | loop fusion | flops 18087936 | bytes 3207232 | tf_op jit(solution)/shard_map/add | solution.py:21
  25.2 1.4 collective-permute-start.1
  26.7 13.2 %fusion.59 = bf16[1,384,1024]{2,1,0:T(8,128)(2,1)S(1)} fusion(f32[384,1024]{1,0:T(8,128)S(1)} %convert_element_type.12, f32[15,1024]{1,0:T(8,128)S(1)} %collective-permute-done, f32[]{:T(128)} %bitcast.15, f32[]{:T(128)} %bitcast.14, f32[]{:T(128)} %bitcast.13, f32[]{:T(128)} %bitcast.12, f32[]{:T(128)} %bitcast.11, f32[]{:T(128)} %bitcast.10, f32[]{:T(128)} %bitcast.9, ...), kind=kLoop, calls=%fused_computation.107 | loop fusion | flops 18481152 | bytes 2420800 | tf_op jit(solution)/shard_map/stack | solution.py:36
  39.9 0.0 collective-permute-done.1
  39.9 13.1 %fusion.60 = bf16[1,384,1024]{2,1,0:T(8,128)(2,1)S(1)} fusion(f32[384,1024]{1,0:T(8,128)S(1)} %multiply_add_fusion, f32[30,1024]{1,0:T(8,128)S(1)} %collective-permute-done.1, f32[]{:T(128)} %bitcast.15, f32[]{:T(128)} %bitcast.14, f32[]{:T(128)} %bitcast.13, f32[]{:T(128)} %bitcast.12, f32[]{:T(128)} %bitcast.11, f32[]{:T(128)} %bitcast.10, f32[]{:T(128)} %bitcast.9, ...), kind=kLoop, calls=%fused_computation.108 | loop fusion | flops 18481152 | bytes 2482240 | tf_op jit(solution)/shard_map/stack | solution.py:36
  53.0 1.3 pad_maximum_fusion.2
  54.3 0.0 all-gather.2.cloned.1.call-update
  54.3 0.0 all-reduce.2.cloned.1.call-start
  54.3 119.1 %all-gather.2.cloned.1.call-done = bf16[2,384,8192]{2,1,0:T(8,128)(2,1)} async-done(((bf16[2,384,1024]{2,1,0:T(8,128)(2,1)}), bf16[2,384,8192]{2,1,0:T(8,128)(2,1)}) %all-gather.2.cloned.1.call-update) | async-done | bytes 12582928 | tf_op jit(solution)/shard_map/all_gather | solution.py:45
  173.4 7.8 multiply_reduce_fusion
  181.2 0.0 all-reduce.2.cloned.1.call-update
  181.2 0.0 reduce-scatter.2.cloned.1.call-start
  181.3 30.2 %convolution_bitcast_fusion = f32[8192,2,1024]{0,2,1:T(8,128)} fusion(bf16[2,384,8192]{2,1,0:T(8,128)(2,1)} %all-gather.2.cloned.1.call-done, bf16[1,384,1024]{2,1,0:T(8,128)(2,1)S(1)} %fusion.60, bf16[1,384,1024]{2,1,0:T(8,128)(2,1)S(1)} %fusion.59), kind=kOutput, calls=%fused_computation | convolution fusion | flops 12885688320 | bytes 81264640 | tf_op jit(solution)/shard_map/jtc,jtr->cjr/dot_general | solution.py:50
  211.5 0.0 reduce-scatter.2.cloned.1.call-update
  211.5 7.8 all-reduce.2.cloned.1.call-done
  219.4 0.7 constant_dynamic-slice_fusion
  220.1 0.7 dynamic-slice_bitcast_fusion
  220.8 560.6 %reduce-scatter.2.cloned.1.call-done = f32[2048,2,1024]{0,2,1:T(8,128)} async-done(((f32[8192,2,1024]{0,2,1:T(8,128)}), f32[2048,2,1024]{0,2,1:T(8,128)}) %reduce-scatter.2.cloned.1.call-update) | async-done | bytes 16777232 | tf_op jit(solution)/shard_map/reduce_scatter | solution.py:49
  781.4 11.9 %subtract_multiply_fusion = f32[2048,2,1024]{0,2,1:T(8,128)} fusion(f32[2048,2,1024]{0,2,1:T(8,128)} %reduce-scatter.2.cloned.1.call-done, f32[2,1024]{1,0:T(2,128)S(1)} %constant_dynamic-slice_fusion, f32[2048,2]{0,1:T(2,128)S(1)} %dynamic-slice_bitcast_fusion), kind=kLoop, calls=%fused_computation.2 | loop fusion | flops 16777216 | bytes 33579008 | tf_op jit(solution)/shard_map/div | solution.py:58
  793.3 25.3 %copy.4 = f32[2048,2,1024]{2,1,0:T(2,128)} copy(f32[2048,2,1024]{0,2,1:T(8,128)} %subtract_multiply_fusion) | data formatting | bytes 33554432 | tf_op jit(solution)/shard_map/div | solution.py:58
  (2 shorter events, 0.0 us)
Async XLA Ops:
  6.5 166.9 %all-gather.2.cloned.1.call-start = ((), (), s32[]{:S(2)}) async-start(), calls=%async_computation.1 | async-start | bytes 14155776 | tf_op jit(solution)/shard_map/all_gather | solution.py:45
  7.3 4.8 collective-permute-start
  25.2 14.7 %collective-permute-start.1 = (f32[30,1024]{1,0:T(8,128)S(1)}, f32[30,1024]{1,0:T(8,128)S(1)}, u32[]{:S(2)}, u32[]{:S(2)}) collective-permute-start(f32[30,1024]{1,0:T(8,128)S(1)} %slice.316), channel_id=1, source_target_pairs={{3,0},{0,1},{1,2},{2,3},{7,4},{4,5},{5,6},{6,7},{11,8},{8,9},{9,10... | collective-permute-start | bytes 368648 | tf_op jit(solution)/shard_map/ppermute | solution.py:13
  54.3 165.1 %all-reduce.2.cloned.1.call-start = ((), (), s32[]{:S(2)}) async-start(), calls=%async_computation.2 | async-start | bytes 131072 | tf_op jit(solution)/shard_map/psum | solution.py:47
  181.2 600.1 %reduce-scatter.2.cloned.1.call-start = ((), (), s32[]{:S(2)}) async-start(), calls=%async_computation.3 | async-start | bytes 83886080 | tf_op jit(solution)/shard_map/reduce_scatter | solution.py:49
Sparse Core Ops, SparseCore 0:
  54.4 118.9 all-gather.1
  181.4 37.9 all-reduce.1
  222.7 558.6 reduce-scatter.1
where the time goes:
time: 829 us; the launch traced here: 825 us
  waiting for transfers between devices  688 us (83%)
  other arithmetic  61.6 us (7%)
  local copies, waits for them, and re-layouts  30.9 us (4%)
  matrix products  30.2 us (4%)
  between operations  13.2 us (2%)
    reduce_scatter x1, waiting for transfers between devices, per_device(): lax.psum_scatter(jnp.einsum('jtc,jtr->cjr', all_coef, own_coef, preferred...  561 us
    all_gather x1, waiting for transfers between devices, per_device(): all_coef = lax.all_gather(own_coef, 'inst', axis=2, tiled=True)  119 us
    dot_general x1, matrix products, per_device(): jnp.einsum('jtc,jtr->cjr', all_coef, own_coef, preferred_element_type=jnp...  30.2 us
    another operation x3, other arithmetic, per_level(): return jnp.stack(details)  27.6 us
    div x1, local copies, waits for them, and re-layouts, per_device(): (jnp.transpose(col_energy)[:, :, None] + row_energy[None, :, :] - 2.0 * g...  25.3 us
  transfers between devices with their start and end apart: 5, of which 3 were waited for; matrix products, arithmetic and copies ran while one was open for 6% of the time, Pallas kernels for 0%

commit v1 on v0

v1 whole, which is shorter than its diff:
```python
import functools

import jax
import jax.numpy as jnp
from jax import lax
from jax.experimental import pallas as pl
from jax.experimental.pallas import tpu as pltpu
from jax.sharding import PartitionSpec as P

TAPS = 16
LEVELS = 2
LAGS = (TAPS - 1) * (2**LEVELS - 1) + 1
HALO = 64
MESH = pl.DeviceIdType.MESH


def chunk_list(slab_rows):
    step = slab_rows // 4
    return [(r, step) for r in range(0, slab_rows, step)]


def gather_kernel(
    tm_size, group_count, chunks,
    x_ref, a_ref, b_ref, z_ref,
    z_send, z_recv, a_send, a_recv, b_send, b_recv, p_send, p_recv, local_sem,
):
    t = lax.axis_index("tm")
    inst = lax.axis_index("inst")
    g = inst // 2
    c = inst % 2
    count = len(chunks)

    barrier = pltpu.get_barrier_semaphore()

    def greet(t2, inst2):
        pl.semaphore_signal(barrier, inc=1, device_id={"tm": t2, "inst": inst2}, device_id_type=MESH)

    pl.when(g > 0)(lambda: greet(t, inst - 2))
    pl.when(g < group_count - 1)(lambda: greet(t, inst + 2))
    greet(t, g * 2 + 1 - c)
    for d in range(1, tm_size):
        greet((t + d) % tm_size, inst)
    expected = tm_size + (g > 0).astype(jnp.int32) + (g < group_count - 1).astype(jnp.int32)
    pl.semaphore_wait(barrier, expected)

    def rows(q):
        return pl.ds(chunks[q][0], chunks[q][1])

    def remote(src, dst, send, recv, t2, inst2):
        return pltpu.make_async_remote_copy(
            src_ref=src, dst_ref=dst, send_sem=send, recv_sem=recv,
            device_id={"tm": t2, "inst": inst2}, device_id_type=MESH,
        )

    def z_copy(k, q, way):
        slab = g - k * way
        src = x_ref if k == 0 else z_ref.at[slab]
        ok = (slab >= 0) & (slab < group_count) & (g + way >= 0) & (g + way < group_count)
        return ok, lambda: remote(
            src.at[rows(q)], z_ref.at[slab, rows(q)],
            z_send.at[(way + 1) // 2, k, q], z_recv.at[slab, q], t, inst + 2 * way,
        )

    def z_arrived(slab, q):
        remote(
            z_ref.at[slab, rows(q)], z_ref.at[slab, rows(q)],
            z_send.at[0, 0, q], z_recv.at[slab, q], t, g * 2 + 1 - c,
        ).wait_recv()

    def a_copy(slab, q):
        return remote(
            z_ref.at[slab, rows(q)], a_ref.at[t, c, rows(q)],
            a_send.at[slab, q], a_recv.at[t, q], slab, inst,
        )

    def a_arrived(s, q):
        remote(
            a_ref.at[s, c, rows(q)], a_ref.at[s, c, rows(q)],
            a_send.at[0, q], a_recv.at[s, q], s, inst,
        ).wait_recv()

    def b_copy(d, q):
        t2 = (t + d) % tm_size
        return remote(
            x_ref.at[rows(q)], b_ref.at[t, rows(q)], b_send.at[d, q], b_recv.at[t, q], t2, inst
        )

    def b_arrived(s, q):
        remote(
            b_ref.at[s, rows(q)], b_ref.at[s, rows(q)], b_send.at[0, q], b_recv.at[s, q], s, inst
        ).wait_recv()

    def p_copy(src, s, q):
        return remote(
            src.at[rows(q)], a_ref.at[s, c, rows(q)],
            p_send.at[s, q], p_recv.at[s, q], t, g * 2 + 1 - c,
        )

    def keep(src, s, q):
        return pltpu.make_async_copy(src.at[rows(q)], a_ref.at[s, c, rows(q)], local_sem.at[s, q])

    own = pltpu.make_async_copy(x_ref, b_ref.at[t], local_sem.at[tm_size, 0])
    own.start()

    def start_if(ok, make):
        pl.when(ok)(lambda: make().start())

    for q in range(count):
        for way in (1, -1):
            start_if(*z_copy(0, q, way))
    own.wait()

    def foreign(slab, q):
        def act():
            z_arrived(slab, q)

        return act

    def handle(k, q):
        for way in (1, -1):
            slab = g - k * way
            have = (slab >= 0) & (slab < group_count)

            @pl.when(have)
            def _():
                z_arrived(slab, q)
                start_if(*z_copy(k, q, way))

                @pl.when(slab != t)
                def _():
                    a_copy(slab, q).start()

                @pl.when(slab == t)
                def _():
                    keep(z_ref.at[slab], t, q).start()
                    p_copy(z_ref.at[slab], t, q).start()

    def settle(q):
        for d in range(1, tm_size):
            s = (t + d) % tm_size
            b_arrived(s, q)

            @pl.when(g == t)
            def _():
                keep(b_ref.at[s], s, q).start()
                p_copy(b_ref.at[s], s, q).start()

            @pl.when(g != t)
            def _():
                a_arrived(s, q)
                p_copy(a_ref.at[s, c], s, q).start()

    for q in range(count):
        for d in range(1, tm_size):
            b_copy(d, q).start()

        @pl.when(g == t)
        def _():
            keep(b_ref.at[t], t, q).start()
            p_copy(b_ref.at[t], t, q).start()

        for k in range(1, group_count):
            handle(k, q)
        if q > 0:
            settle(q - 1)
    settle(count - 1)

    for q in range(count):
        for s in range(tm_size):
            remote(
                a_ref.at[s, 1 - c, rows(q)], a_ref.at[s, 1 - c, rows(q)],
                p_send.at[s, q], p_recv.at[s, q], t, g * 2 + 1 - c,
            ).wait_recv()
            p_copy(x_ref, s, q).wait_send()
            pl.when((g == t) | (s == t))(lambda: keep(x_ref, s, q).wait())
        for k in range(group_count):
            for way in (1, -1):
                ok, make = z_copy(k, q, way)
                pl.when(ok)(lambda: make().wait_send())
        for slab in range(group_count):
            pl.when((slab != g) & (slab != t))(lambda: a_copy(slab, q).wait_send())
        for d in range(1, tm_size):
            b_copy(d, q).wait_send()


def gather(log_prices, tm_size, inst_size):
    slab_rows, cols = log_prices.shape
    group_count = inst_size // 2
    chunks = chunk_list(slab_rows)
    n = len(chunks)
    dma = pltpu.SemaphoreType.DMA
    vmem = pl.BlockSpec(memory_space=pltpu.VMEM)
    return pl.pallas_call(
        functools.partial(gather_kernel, tm_size, group_count, chunks),
        out_shape=[
            jax.ShapeDtypeStruct((tm_size, 2, slab_rows, cols), jnp.bfloat16),
            jax.ShapeDtypeStruct((tm_size, slab_rows, cols), jnp.bfloat16),
        ],
        in_specs=[vmem],
        out_specs=[vmem, vmem],
        scratch_shapes=[
            pltpu.VMEM((group_count, slab_rows, cols), jnp.bfloat16),
            dma((2, group_count, n)), dma((group_count, n)),
            dma((group_count, n)), dma((tm_size, n)),
            dma((tm_size, n)), dma((tm_size, n)),
            dma((tm_size, n)), dma((tm_size, n)),
            dma((tm_size + 1, n)),
        ],
        compiler_params=pltpu.CompilerParams(
            collective_id=0, has_side_effects=True, vmem_limit_bytes=40 * 2**20
        ),
        name="gather_series",
    )(log_prices)


def build_bands(f_ref, band_ref):
    half = band_ref.shape[0] // 4
    low = [f_ref[l] for l in range(TAPS)]
    high = [(-1.0) ** l * low[TAPS - 1 - l] for l in range(TAPS)]
    joint = [None] * LAGS
    for b in range(TAPS):
        for l in range(TAPS):
            term = low[l] * high[b]
            lag = l + 2 * b
            joint[lag] = term if joint[lag] is None else joint[lag] + term
    shape = (half, HALO + half)
    lag = HALO + lax.broadcasted_iota(jnp.int32, shape, 0) - lax.broadcasted_iota(jnp.int32, shape, 1)
    for level, taps in enumerate((high, joint)):
        band = jnp.zeros(shape, jnp.float32)
        for l, weight in enumerate(taps):
            band = jnp.where(lag == l, weight, band)
        head = band.astype(jnp.bfloat16)
        rest = (band - head.astype(jnp.float32)).astype(jnp.bfloat16)
        band_ref[pl.ds(level * half, half), :] = head
        band_ref[pl.ds((2 + level) * half, half), :] = rest


def coefficients(band_ref, window):
    half = band_ref.shape[0] // 4
    both = jnp.dot(band_ref[...], window, preferred_element_type=jnp.float32)
    total = (both[: 2 * half] + both[2 * half :]).astype(jnp.bfloat16)
    return total[:half], total[half:]


def gram_kernel(tm_size, f_ref, a_ref, b_ref, o_ref, band_ref, ca_ref, cb_ref, eb_ref):
    slab_rows = b_ref.shape[1]
    half = slab_rows // 2
    width = a_ref.shape[3]
    cols = b_ref.shape[2]
    ticks = tm_size * slab_rows

    def sweep(load, c_ref, where):
        def slab(s, sums):
            before = (s + tm_size - 1) % tm_size
            sums = list(sums)
            windows = (
                jnp.concatenate(
                    [load(before, slab_rows - HALO, HALO), load(s, 0, half)], 0
                ),
                load(s, half - HALO, HALO + half),
            )
            for h, window in enumerate(windows):
                first = pl.multiple_of(s * slab_rows + h * half, half)
                for level, part in enumerate(coefficients(band_ref, window)):
                    c_ref[level, pl.ds(first, half), where] = part
                    wide = part.astype(jnp.float32)
                    sums[level] = sums[level] + jnp.sum(wide * wide, axis=0, keepdims=True)
            return tuple(sums)

        zero = jnp.zeros((1, width), jnp.float32)
        return lax.fori_loop(0, tm_size, slab, (zero, zero))

    @pl.when(pl.program_id(0) == 0)
    def _():
        build_bands(f_ref, band_ref)
        for n in range(cols // width):
            where = pl.ds(n * width, width)
            sums = sweep(lambda s, r, m: b_ref[s, pl.ds(r, m), where], cb_ref, where)
            for level in range(LEVELS):
                eb_ref[pl.ds(level, 1), where] = sums[level]

    sums = sweep(lambda s, r, m: a_ref[s, 0, pl.ds(r, m), :], ca_ref, pl.ds(0, width))
    for level in range(LEVELS):
        gram = lax.dot_general(
            ca_ref[level], cb_ref[level], (((0,), (0,)), ((), ())),
            preferred_element_type=jnp.float32,
        )
        column = jnp.transpose(jnp.broadcast_to(sums[level], (8, width)))[:, :1]
        row = eb_ref[pl.ds(level, 1), :]
        o_ref[:, level, :] = (column + row - 2.0 * gram) * (1.0 / ticks)


def variation(scaling_filter, a, b):
    tm_size, _, slab_rows, cols = a.shape
    ticks = tm_size * slab_rows
    width = 256
    per_half = cols // width
    half = slab_rows // 2
    return pl.pallas_call(
        functools.partial(gram_kernel, tm_size),
        grid=(2 * per_half,),
        out_shape=jax.ShapeDtypeStruct((2 * cols, LEVELS, cols), jnp.float32),
        in_specs=[
            pl.BlockSpec(memory_space=pltpu.SMEM),
            pl.BlockSpec((tm_size, 1, slab_rows, width), lambda n: (0, n // per_half, 0, n % per_half)),
            pl.BlockSpec((tm_size, slab_rows, cols), lambda n: (0, 0, 0)),
        ],
        out_specs=pl.BlockSpec((width, LEVELS, cols), lambda n: (n, 0, 0)),
        scratch_shapes=[
            pltpu.VMEM((4 * half, HALO + half), jnp.bfloat16),
            pltpu.VMEM((LEVELS, ticks, width), jnp.bfloat16),
            pltpu.VMEM((LEVELS, ticks, cols), jnp.bfloat16),
            pltpu.VMEM((8, cols), jnp.float32),
        ],
        compiler_params=pltpu.CompilerParams(vmem_limit_bytes=48 * 2**20),
        name="variation_tiles",
    )(scaling_filter, a, b)


def solution(mesh):
    tm_size, inst_size = mesh.shape["tm"], mesh.shape["inst"]

    def per_device(log_prices, scaling_filter):
        a, b = gather(log_prices, tm_size, inst_size)
        return variation(scaling_filter, a, b)

    placed = (P("tm", "inst"), P())
    return jax.shard_map(
        per_device, mesh=mesh, in_specs=placed, out_specs=P("tm", None, "inst"), check_vma=False
    )
```

time: 829 us -> 138 us (0.17)
  waiting for transfers between devices: 688 us -> 0 us
  Pallas kernels: 0 us -> 133 us
  other arithmetic: 61.6 us -> 0 us
  matrix products: 30.2 us -> 0 us
  local copies, waits for them, and re-layouts: 30.9 us -> 4.42 us
  between operations: 13.2 us -> 0.02 us
    reduce_scatter x1 -> x0, waiting for transfers between devices: 561 us -> none  [per_device(): lax.psum_scatter(jnp.einsum('jtc,jtr->cjr', all_coef, own_coef, preferred...]
    pallas_call x0 -> x2, Pallas kernels: none -> 133 us  [the longest x1 92.3 us: gather(): pl.pallas_call(functools.partial(gather_kernel, tm_size, group_count, chu...]
    all_gather x1 -> x0, waiting for transfers between devices: 119 us -> none  [per_device(): all_coef = lax.all_gather(own_coef, 'inst', axis=2, tiled=True)]
    dot_general x1 -> x0, matrix products: 30.2 us -> none  [per_device(): jnp.einsum('jtc,jtr->cjr', all_coef, own_coef, preferred_element_type=jnp...]
    another operation x3 -> x0, other arithmetic: 27.6 us -> none  [per_level(): return jnp.stack(details)]
    div x1 -> x0, local copies, waits for them, and re-layouts: 25.3 us -> none  [per_device(): (jnp.transpose(col_energy)[:, :, None] + row_energy[None, :, :] - 2.0 * g...]
    add x1 -> x0, other arithmetic: 13.1 us -> none  [apply_taps(): running + filter_taps[lag_index] * extended[first_row:first_row + row_count]]
    div x1 -> x0, other arithmetic: 11.9 us -> none  [per_device(): (jnp.transpose(col_energy)[:, :, None] + row_energy[None, :, :] - 2.0 * g...]
  transfers between devices with their start and end apart: 5 -> 0, of which waited for: 3 -> 0; matrix products, arithmetic and copies ran while one was open for 6% -> 0% of each run, Pallas kernels for 0% -> 0%
where the time goes in v1:
time: 138 us; the launch traced here: 137 us
  Pallas kernels  133 us (96%)
  local copies, waits for them, and re-layouts  4.42 us (3%)
    pallas_call x1, Pallas kernels, gather(): pl.pallas_call(functools.partial(gather_kernel, tm_size, group_count, chu...  92.3 us
    pallas_call x1, Pallas kernels, variation(): pl.pallas_call(functools.partial(gram_kernel, tm_size), grid=(2 * per_hal...  40.6 us
    unnamed x6, local copies, waits for them, and re-layouts  4.42 us

profile of v1, /device:TPU:7, one launch (start us, length us, event | category | flops | bytes accessed | tf_op | source)
XLA Modules:
  0.0 137.3 jit_solution(17780246243274530860)
XLA Ops:
  0.0 0.0 copy-start.1
  0.0 1.1 copy-done.1
  1.1 92.3 %gather_series.1 = (bf16[4,2,384,1024]{3,2,1,0:T(8,128)(2,1)S(1)}, bf16[4,384,1024]{2,1,0:T(8,128)(2,1)S(1)}) custom-call(bf16[384,1024]{1,0:T(8,128)(2,1)S(1)} %copy-done.1), custom_call_target="tpu_custom_call" | custom-call | tf_op jit(solution)/shard_map/gather_series/pallas_call | solution.py:193
  93.5 0.0 copy-start
  93.5 2.6 %copy-done = bf16[4,2,384,1024]{3,2,1,0:T(8,128)(2,1)} copy-done((bf16[4,2,384,1024]{3,2,1,0:T(8,128)(2,1)}, bf16[4,2,384,1024]{3,2,1,0:T(8,128)(2,1)S(1)}, u32[]{:S(2)}) %copy-start) | copy-done | bytes 6291480
  96.1 0.0 copy-start.2
  96.1 0.7 copy-done.2
  96.8 40.6 %variation_tiles.1 = f32[2048,2,1024]{2,1,0:T(2,128)} custom-call(f32[16]{0:T(128)S(1)} %copy-done.2, bf16[4,2,384,1024]{3,2,1,0:T(8,128)(2,1)} %copy-done, bf16[4,384,1024]{2,1,0:T(8,128)(2,1)S(1)} %get-tuple-element.8.b_ref), custom_call_target="tpu_custom_call" | custom-call | tf_op jit(solution)/shard_map/variation_tiles/pallas_call | solution.py:299
Async XLA Ops:
  0.0 1.1 copy-start.1
  93.5 2.6 %copy-start = (bf16[4,2,384,1024]{3,2,1,0:T(8,128)(2,1)}, bf16[4,2,384,1024]{3,2,1,0:T(8,128)(2,1)S(1)}, u32[]{:S(2)}) copy-start(bf16[4,2,384,1024]{3,2,1,0:T(8,128)(2,1)S(1)} %get-tuple-element.7.a_ref) | copy-start | bytes 18874372
  96.1 0.7 copy-start.2
